TPU v7x, 256 devices: a whole 4x4x8 slice. The times are simulated.
256 devices in a mesh: frames: 16 (over z_lo, y, core), heads: 16 (over x, z_hi).
Axes of the slice: x: 4, y: 4, z: 8 (z_hi: 4, z_lo: 2; z = z_hi * 2 + z_lo), core: 2. Of those that a mesh axis runs over, the one named last changes fastest.
Arguments:
- query_spatial: bfloat16 [32, 1024, 2048], P('frames', None, 'heads'), may hold values from -6 to 6
- key_spatial: bfloat16 [32, 1024, 2048], P('frames', None, 'heads'), may hold values from -6 to 6
- value_spatial: bfloat16 [32, 1024, 2048], P('frames', None, 'heads'), may hold values from -6 to 6
- output_spatial: bfloat16 [32, 1024, 2048], P('frames', None, 'heads'), may hold values from -6 to 6
- grad_spatial: bfloat16 [32, 1024, 2048], P('frames', None, 'heads'), may hold values from -96 to 96
- query_temporal: bfloat16 [2, 16, 1024, 2048], P(None, 'frames', None, 'heads'), may hold values from -6 to 6
- key_temporal: bfloat16 [2, 16, 1024, 2048], P(None, 'frames', None, 'heads'), may hold values from -6 to 6
- value_temporal: bfloat16 [2, 16, 1024, 2048], P(None, 'frames', None, 'heads'), may hold values from -6 to 6
- output_temporal: bfloat16 [2, 16, 1024, 2048], P(None, 'frames', None, 'heads'), may hold values from -6 to 6
- grad_temporal: bfloat16 [2, 16, 1024, 2048], P(None, 'frames', None, 'heads'), may hold values from -12 to 12
Outputs:
- dquery_spatial: bfloat16 [32, 1024, 2048], P('frames', None, 'heads')
- dkey_spatial: bfloat16 [32, 1024, 2048], P('frames', None, 'heads')
- dvalue_spatial: bfloat16 [32, 1024, 2048], P('frames', None, 'heads')
- dquery_temporal: bfloat16 [2, 16, 1024, 2048], P(None, 'frames', None, 'heads')
- dkey_temporal: bfloat16 [2, 16, 1024, 2048], P(None, 'frames', None, 'heads')
- dvalue_temporal: bfloat16 [2, 16, 1024, 2048], P(None, 'frames', None, 'heads')
All inputs are finite; a program needn't handle non-finite values.
Results may differ from a plain program's by a relative error of at most 0.0054.
Values may be sent and summed in bfloat16 or wider, within the bound.
A program may use at most 64 MiB of HBM per device.

v0:
```python
import jax
import jax.numpy as jnp
from jax import lax
from jax.sharding import PartitionSpec as P

HD = 128


def spatial_grads(queries, key_rows, value_rows, output_rows, grad_rows):
    frames, tokens, channels = queries.shape
    head_count = channels // HD
    shape = (frames, tokens, head_count, HD)
    query_heads = queries.reshape(shape)
    key_heads = key_rows.reshape(shape)
    value_heads = value_rows.reshape(shape)
    output_heads = output_rows.reshape(shape)
    grad_heads = grad_rows.reshape(shape)
    scaling = HD ** (-0.5)
    scores = (
        jnp.einsum("fqhd,fkhd->fhqk", query_heads, key_heads, preferred_element_type=jnp.float32)
        * scaling
    )
    weights = jax.nn.softmax(scores, axis=-1)
    weights_low = weights.astype(jnp.bfloat16)
    grad_value = jnp.einsum(
        "fhqk,fqhd->fkhd", weights_low, grad_heads, preferred_element_type=jnp.float32
    ).astype(jnp.bfloat16)
    grad_weight = jnp.einsum(
        "fqhd,fkhd->fhqk", grad_heads, value_heads, preferred_element_type=jnp.float32
    )
    row_dot = jnp.sum(grad_heads.astype(jnp.float32) * output_heads.astype(jnp.float32), axis=-1)
    row_dot = jnp.transpose(row_dot, (0, 2, 1))
    grad_low = (weights * (grad_weight - row_dot[..., None])).astype(jnp.bfloat16)
    grad_query = (
        jnp.einsum("fhqk,fkhd->fqhd", grad_low, key_heads, preferred_element_type=jnp.float32)
        * scaling
    ).astype(jnp.bfloat16)
    grad_key = (
        jnp.einsum("fhqk,fqhd->fkhd", grad_low, query_heads, preferred_element_type=jnp.float32)
        * scaling
    ).astype(jnp.bfloat16)
    final = (frames, tokens, channels)
    return (grad_query.reshape(final), grad_key.reshape(final), grad_value.reshape(final))


def temporal_grads(queries, key_rows, value_rows, grad_rows, row_stats):
    clip_count, clip_len, columns, channels = queries.shape
    group = channels // HD
    shape = (clip_count, clip_len, columns, group, HD)
    query_heads = queries.reshape(shape)
    key_heads = key_rows.reshape(shape)
    value_heads = value_rows.reshape(shape)
    grad_heads = grad_rows.reshape(shape)
    scaling = HD ** (-0.5)
    scores = (
        jnp.einsum("cqxyd,ckxyd->cxyqk", query_heads, key_heads, preferred_element_type=jnp.float32)
        * scaling
    )
    weights = jax.nn.softmax(scores, axis=-1)
    weights_low = weights.astype(jnp.bfloat16)
    grad_value = jnp.einsum(
        "cxyqk,cqxyd->ckxyd", weights_low, grad_heads, preferred_element_type=jnp.float32
    ).astype(jnp.bfloat16)
    grad_weight = jnp.einsum(
        "cqxyd,ckxyd->cxyqk", grad_heads, value_heads, preferred_element_type=jnp.float32
    )
    row_dot = jnp.moveaxis(row_stats.astype(jnp.float32), 1, -1)
    grad_low = (weights * (grad_weight - row_dot[..., None])).astype(jnp.bfloat16)
    grad_query = (
        jnp.einsum("cxyqk,ckxyd->cqxyd", grad_low, key_heads, preferred_element_type=jnp.float32)
        * scaling
    ).astype(jnp.bfloat16)
    grad_key = (
        jnp.einsum("cxyqk,cqxyd->ckxyd", grad_low, query_heads, preferred_element_type=jnp.float32)
        * scaling
    ).astype(jnp.bfloat16)
    final = (clip_count, clip_len, columns, channels)
    return (grad_query.reshape(final), grad_key.reshape(final), grad_value.reshape(final))


def row_statistic(grad_rows, output_rows):
    clip_count, frames, columns, channels = grad_rows.shape
    products = grad_rows.astype(jnp.float32) * output_rows.astype(jnp.float32)
    return jnp.sum(
        products.reshape(clip_count, frames, columns, channels // HD, HD), axis=-1
    ).astype(jnp.bfloat16)


def body(
    query_spatial,
    key_spatial,
    value_spatial,
    output_spatial,
    grad_spatial,
    query_temporal,
    key_temporal,
    value_temporal,
    output_temporal,
    grad_temporal,
):
    spatial = spatial_grads(query_spatial, key_spatial, value_spatial, output_spatial, grad_spatial)
    row_stats = row_statistic(grad_temporal, output_temporal)
    payload = (query_temporal, key_temporal, value_temporal, grad_temporal, row_stats)
    arrived = (
        lax.all_to_all(payload[0], "frames", split_axis=2, concat_axis=1, tiled=True),
        lax.all_to_all(payload[1], "frames", split_axis=2, concat_axis=1, tiled=True),
        lax.all_to_all(payload[2], "frames", split_axis=2, concat_axis=1, tiled=True),
        lax.all_to_all(payload[3], "frames", split_axis=2, concat_axis=1, tiled=True),
        lax.all_to_all(payload[4], "frames", split_axis=2, concat_axis=1, tiled=True),
    )
    temporal_query, temporal_key, temporal_value, temporal_grad, temporal_extra = arrived
    gradients = temporal_grads(
        temporal_query, temporal_key, temporal_value, temporal_grad, temporal_extra
    )
    returned = (
        lax.all_to_all(gradients[0], "frames", split_axis=1, concat_axis=2, tiled=True),
        lax.all_to_all(gradients[1], "frames", split_axis=1, concat_axis=2, tiled=True),
        lax.all_to_all(gradients[2], "frames", split_axis=1, concat_axis=2, tiled=True),
    )
    return (spatial[0], spatial[1], spatial[2], returned[0], returned[1], returned[2])


def solution(mesh):
    in_specs = (
        P("frames", None, "heads"),
        P("frames", None, "heads"),
        P("frames", None, "heads"),
        P("frames", None, "heads"),
        P("frames", None, "heads"),
        P(None, "frames", None, "heads"),
        P(None, "frames", None, "heads"),
        P(None, "frames", None, "heads"),
        P(None, "frames", None, "heads"),
        P(None, "frames", None, "heads"),
    )
    out_specs = (
        P("frames", None, "heads"),
        P("frames", None, "heads"),
        P("frames", None, "heads"),
        P(None, "frames", None, "heads"),
        P(None, "frames", None, "heads"),
        P(None, "frames", None, "heads"),
    )
    return jax.shard_map(body, mesh=mesh, in_specs=in_specs, out_specs=out_specs, check_vma=False)
```

profile of v0, /device:TPU:1, one launch (start us, length us, event | category | flops | bytes accessed | tf_op | source)
XLA Modules:
  0.0 131.2 jit_solution(4275764479012620913)
XLA Ops:
  0.6 0.0 copy-start
  0.7 1.6 %multiply_reduce_fusion.1 = bf16[2,1024]{1,0:T(2,128)(2,1)S(1)} fusion(bf16[2,1,1024,128]{3,2,1,0:T(8,128)(2,1)} %param.18, bf16[2,1,1024,128]{3,2,1,0:T(8,128)(2,1)} %param.19), kind=kLoop, calls=%fused_computation.29 | loop fusion | flops 1046528 | bytes 1052672 | tf_op jit(solution)/shard_map/reduce_sum | solution.py:84
  2.3 1.1 copy.117
  3.4 7.3 %all-to-all-start.4 = ((bf16[2,1,1024,1]{0,3,1,2:T(2,128)(2,1)}), bf16[2,1,1024,1]{0,3,1,2:T(2,128)(2,1)S(1)}, u32[]{:S(2)}, u32[]{:S(2)}) async-start(bf16[2,1,1024,1]{0,3,1,2:T(2,128)(2,1)} %copy.117), calls=%async_computation.4 | async-start | bytes 1048576 | tf_op jit(solution)/shard_map/all_to_all | solution.py:109
  10.8 2.4 %copy.111 = bf16[2,1,1024,128]{3,0,1,2:T(2,128)(2,1)} copy(bf16[2,1,1024,128]{3,2,1,0:T(8,128)(2,1)} %param.19) | data formatting | bytes 1048576 | tf_op args[9]
  13.2 7.4 %all-to-all-done.4 = bf16[2,1,1024,1]{0,3,1,2:T(2,128)(2,1)S(1)} async-done(((bf16[2,1,1024,1]{0,3,1,2:T(2,128)(2,1)}), bf16[2,1,1024,1]{0,3,1,2:T(2,128)(2,1)S(1)}, u32[]{:S(2)}, u32[]{:S(2)}) %all-to-all-start.4) | async-done | bytes 4128 | tf_op jit(solution)/shard_map/all_to_all | solution.py:109
  20.6 4.5 %all-to-all-start.2 = ((bf16[2,1,1024,128]{3,0,1,2:T(2,128)(2,1)}), bf16[2,1,1024,128]{3,0,1,2:T(2,128)(2,1)S(1)}, u32[]{:S(2)}, u32[]{:S(2)}) async-start(bf16[2,1,1024,128]{3,0,1,2:T(2,128)(2,1)} %copy.111), calls=%async_computation.2 | async-start | bytes 1048576 | tf_op jit(solution)/shard_map/all_to_all | solution.py:108
  25.1 2.4 %copy.107 = bf16[2,1,1024,128]{3,0,1,2:T(2,128)(2,1)} copy(bf16[2,1,1024,128]{3,2,1,0:T(8,128)(2,1)} %param.16) | data formatting | bytes 1048576 | tf_op args[6]
  27.5 7.5 %all-to-all-done.2 = bf16[2,1,1024,128]{3,0,1,2:T(2,128)(2,1)S(1)} async-done(((bf16[2,1,1024,128]{3,0,1,2:T(2,128)(2,1)}), bf16[2,1,1024,128]{3,0,1,2:T(2,128)(2,1)S(1)}, u32[]{:S(2)}, u32[]{:S(2)}) %all-to-all-start.2) | async-done | bytes 524320 | tf_op jit(solution)/shard_map/all_to_all | solution.py:108
  35.0 4.5 %all-to-all-start.1 = ((bf16[2,1,1024,128]{3,0,1,2:T(2,128)(2,1)}), bf16[2,1,1024,128]{3,0,1,2:T(2,128)(2,1)S(1)}, u32[]{:S(2)}, u32[]{:S(2)}) async-start(bf16[2,1,1024,128]{3,0,1,2:T(2,128)(2,1)} %copy.107), calls=%async_computation.1 | async-start | bytes 1048576 | tf_op jit(solution)/shard_map/all_to_all | solution.py:106
  39.5 2.4 %copy.105 = bf16[2,1,1024,128]{3,0,1,2:T(2,128)(2,1)} copy(bf16[2,1,1024,128]{3,2,1,0:T(8,128)(2,1)} %param.15) | data formatting | bytes 1048576 | tf_op args[5]
  41.9 7.5 %all-to-all-done.1 = bf16[2,1,1024,128]{3,0,1,2:T(2,128)(2,1)S(1)} async-done(((bf16[2,1,1024,128]{3,0,1,2:T(2,128)(2,1)}), bf16[2,1,1024,128]{3,0,1,2:T(2,128)(2,1)S(1)}, u32[]{:S(2)}, u32[]{:S(2)}) %all-to-all-start.1) | async-done | bytes 524320 | tf_op jit(solution)/shard_map/all_to_all | solution.py:106
  49.4 4.5 %all-to-all-start = ((bf16[2,1,1024,128]{3,0,1,2:T(2,128)(2,1)}), bf16[2,1,1024,128]{3,0,1,2:T(2,128)(2,1)S(1)}, u32[]{:S(2)}, u32[]{:S(2)}) async-start(bf16[2,1,1024,128]{3,0,1,2:T(2,128)(2,1)} %copy.105), calls=%async_computation | async-start | bytes 1048576 | tf_op jit(solution)/shard_map/all_to_all | solution.py:105
  53.9 1.3 %copy.113 = bf16[2,1,1024,128]{3,0,1,2:T(2,128)(2,1)} copy(bf16[2,1,1024,128]{3,2,1,0:T(8,128)(2,1)S(1)} %copy-done.1) | data formatting | bytes 1048576 | tf_op args[7]
  55.3 8.5 %all-to-all-done = bf16[2,1,1024,128]{3,0,1,2:T(2,128)(2,1)S(1)} async-done(((bf16[2,1,1024,128]{3,0,1,2:T(2,128)(2,1)}), bf16[2,1,1024,128]{3,0,1,2:T(2,128)(2,1)S(1)}, u32[]{:S(2)}, u32[]{:S(2)}) %all-to-all-start) | async-done | bytes 524320 | tf_op jit(solution)/shard_map/all_to_all | solution.py:105
  63.8 5.1 %all-to-all-start.3 = ((bf16[2,1,1024,128]{3,0,1,2:T(2,128)(2,1)}), bf16[2,1,1024,128]{3,0,1,2:T(2,128)(2,1)}, u32[]{:S(2)}, u32[]{:S(2)}) async-start(bf16[2,1,1024,128]{3,0,1,2:T(2,128)(2,1)} %copy.113), calls=%async_computation.3 | async-start | bytes 1048576 | tf_op jit(solution)/shard_map/all_to_all | solution.py:107
  69.0 1.5 %multiply_reduce_fusion.2 = f32[2,1024]{1,0:T(2,128)S(1)} fusion(bf16[2,1024,128]{2,1,0:T(8,128)(2,1)} %param.13, bf16[2,1024,128]{2,1,0:T(8,128)(2,1)} %param.14), kind=kLoop, calls=%fused_computation.30 | loop fusion | flops 1046528 | bytes 1056768 | tf_op jit(solution)/shard_map/reduce_sum | solution.py:31
  70.5 0.0 copy-done
  70.5 7.0 %fusion.43 = (f32[2,1024]{1,0:T(2,128)S(1)}, f32[2,1024,1024]{1,2,0:T(8,128)}) fusion(bf16[2,1024,128]{2,1,0:T(8,128)(2,1)} %param.10, bf16[2,1024,128]{2,1,0:T(8,128)(2,1)S(1)} %copy-done), kind=kOutput, calls=%fused_computation.45 | convolution fusion | flops 543163392 | bytes 9445376 | tf_op jit(solution)/shard_map/sub | solution.py:23
  77.5 0.3 copy.118
  77.8 0.1 reshape.214
  77.9 0.1 copy.119
  78.0 0.9 copy.112
  78.9 0.1 copy.108
  78.9 0.1 copy.106
  79.0 1.0 fusion.44
  80.0 0.0 all-to-all-done.3
  80.0 2.6 %fusion.11 = bf16[2,64,16,16]{2,3,1,0:T(8,128)(2,1)S(1)} fusion(bf16[2,16,64,128]{3,0,2,1:T(2,128)(2,1)} %bitcast.3, f32[2,64,16]{2,1,0:T(8,128)S(1)} %copy.119, bf16[2,16,64,128]{3,2,1,0:T(8,128)(2,1)} %bitcast.62, f32[2,64,16,16]{2,3,1,0:T(8,128)S(1)} %get-tuple-element.33, f32[2,64,16]{2,1,0:T(8,128)S(1)} %get-tuple-element.32), kind=kOutput, calls=%fused_computation.19 | convolution fusion | flops 8519680 | bytes 1261568 | tf_op jit(solution)/shard_map/cqxyd,ckxyd->cxyqk/dot_general | solution.py:64
  82.6 0.5 fusion.20
  83.1 0.9 copy.123
  84.1 5.8 %all-to-all-start.5 = ((bf16[2,16,64,128]{3,2,0,1:T(8,128)(2,1)}), bf16[2,16,64,128]{3,2,0,1:T(8,128)(2,1)S(1)}, u32[]{:S(2)}, u32[]{:S(2)}) async-start(bf16[2,16,64,128]{3,2,0,1:T(8,128)(2,1)} %copy.123), calls=%async_computation.5 | async-start | bytes 1048576 | tf_op jit(solution)/shard_map/all_to_all | solution.py:116
  89.9 6.9 %multiply_convert_fusion = bf16[2,1024,1024]{1,2,0:T(8,128)(2,1)} fusion(f32[2,1024]{1,0:T(2,128)S(1)} %multiply_reduce_fusion.2, f32[2,1024,1024]{1,2,0:T(8,128)} %get-tuple-element.31, f32[2,1024]{1,0:T(2,128)S(1)} %get-tuple-element.30, bf16[2,1024,128]{2,1,0:T(8,128)(2,1)} %param.14, bf16[2,1024,128]{2,1,0:T(8,128)(2,1)} %param.12), kind=kOutput, calls=%fused_computation.2 | convolution fusion | flops 545259520 | bytes 13647872 | tf_op jit(solution)/shard_map/fqhd,fkhd->fhqk/dot_general | solution.py:28
  96.8 0.5 fusion.19
  97.3 0.9 copy.126
  98.3 1.4 %all-to-all-done.5 = bf16[2,16,64,128]{3,2,0,1:T(8,128)(2,1)S(1)} async-done(((bf16[2,16,64,128]{3,2,0,1:T(8,128)(2,1)}), bf16[2,16,64,128]{3,2,0,1:T(8,128)(2,1)S(1)}, u32[]{:S(2)}, u32[]{:S(2)}) %all-to-all-start.5) | async-done | bytes 524320 | tf_op jit(solution)/shard_map/all_to_all | solution.py:116
  99.7 4.5 %all-to-all-start.6 = ((bf16[2,16,64,128]{3,2,0,1:T(8,128)(2,1)}), bf16[2,16,64,128]{3,2,0,1:T(8,128)(2,1)S(1)}, u32[]{:S(2)}, u32[]{:S(2)}) async-start(bf16[2,16,64,128]{3,2,0,1:T(8,128)(2,1)} %copy.126), calls=%async_computation.6 | async-start | bytes 1048576 | tf_op jit(solution)/shard_map/all_to_all | solution.py:117
  104.2 0.0 copy-start.2
  104.2 4.8 %fusion.15 = bf16[2,1024,128]{2,1,0:T(8,128)(2,1)} fusion(bf16[2,1024,1024]{1,2,0:T(8,128)(2,1)} %multiply_convert_fusion, bf16[2,1024,128]{2,1,0:T(8,128)(2,1)S(1)} %copy-done), kind=kOutput, calls=%fused_computation.22 | convolution fusion | flops 537395200 | bytes 5242880 | tf_op jit(solution)/shard_map/fhqk,fkhd->fqhd/dot_general | solution.py:35
  109.0 4.2 %fusion.16 = bf16[2,1024,128]{2,1,0:T(8,128)(2,1)} fusion(bf16[2,1024,1024]{1,2,0:T(8,128)(2,1)} %multiply_convert_fusion, bf16[2,1024,128]{2,1,0:T(8,128)(2,1)S(1)} %copy-done.4), kind=kOutput, calls=%fused_computation.23 | convolution fusion | flops 537395200 | bytes 5242880 | tf_op jit(solution)/shard_map/fhqk,fqhd->fkhd/dot_general | solution.py:39
  113.3 0.5 fusion.21
  113.8 0.9 copy.129
  114.7 0.0 all-to-all-done.6
  114.7 5.8 %all-to-all-start.7 = ((bf16[2,16,64,128]{3,2,0,1:T(8,128)(2,1)}), bf16[2,16,64,128]{3,2,0,1:T(8,128)(2,1)S(1)}, u32[]{:S(2)}, u32[]{:S(2)}) async-start(bf16[2,16,64,128]{3,2,0,1:T(8,128)(2,1)} %copy.129), calls=%async_computation.7 | async-start | bytes 1048576 | tf_op jit(solution)/shard_map/all_to_all | solution.py:118
  120.5 5.4 %fusion.12 = bf16[2,1024,128]{2,1,0:T(8,128)(2,1)} fusion(bf16[2,1024,128]{2,1,0:T(8,128)(2,1)S(1)} %copy-done.2, f32[2,1024,1024]{1,2,0:T(8,128)} %get-tuple-element.31, f32[2,1024]{1,0:T(2,128)S(1)} %get-tuple-element.30), kind=kOutput, calls=%fused_computation.20 | convolution fusion | flops 541327360 | bytes 9445376 | tf_op jit(solution)/shard_map/fhqk,fqhd->fkhd/dot_general | solution.py:25
  126.0 0.8 copy.124
  126.8 0.8 copy.127
  127.6 2.7 %all-to-all-done.7 = bf16[2,16,64,128]{3,2,0,1:T(8,128)(2,1)S(1)} async-done(((bf16[2,16,64,128]{3,2,0,1:T(8,128)(2,1)}), bf16[2,16,64,128]{3,2,0,1:T(8,128)(2,1)S(1)}, u32[]{:S(2)}, u32[]{:S(2)}) %all-to-all-start.7) | async-done | bytes 524320 | tf_op jit(solution)/shard_map/all_to_all | solution.py:118
  130.3 0.8 copy.130
  (11 shorter events, 0.0 us)
Async XLA Ops:
  0.6 69.9 %copy-start = (bf16[2,1024,128]{2,1,0:T(8,128)(2,1)S(1)}, bf16[2,1024,128]{2,1,0:T(8,128)(2,1)}, u32[]{:S(2)}) copy-start(bf16[2,1024,128]{2,1,0:T(8,128)(2,1)} %param.11) | copy-start | bytes 1572868
  0.6 53.3 %copy-start.1 = (bf16[2,1,1024,128]{3,2,1,0:T(8,128)(2,1)S(1)}, bf16[2,1,1024,128]{3,2,1,0:T(8,128)(2,1)}, u32[]{:S(2)}) copy-start(bf16[2,1,1024,128]{3,2,1,0:T(8,128)(2,1)} %param.17) | copy-start | bytes 1572868
  3.4 17.1 %all-to-all-start.4 = ((bf16[2,1,1024,1]{0,3,1,2:T(2,128)(2,1)}), bf16[2,1,1024,1]{0,3,1,2:T(2,128)(2,1)S(1)}, u32[]{:S(2)}, u32[]{:S(2)}) async-start(bf16[2,1,1024,1]{0,3,1,2:T(2,128)(2,1)} %copy.117), calls=%async_computation.4 | async-start | bytes 1048576 | tf_op jit(solution)/shard_map/all_to_all | solution.py:109
  20.6 14.4 %all-to-all-start.2 = ((bf16[2,1,1024,128]{3,0,1,2:T(2,128)(2,1)}), bf16[2,1,1024,128]{3,0,1,2:T(2,128)(2,1)S(1)}, u32[]{:S(2)}, u32[]{:S(2)}) async-start(bf16[2,1,1024,128]{3,0,1,2:T(2,128)(2,1)} %copy.111), calls=%async_computation.2 | async-start | bytes 1048576 | tf_op jit(solution)/shard_map/all_to_all | solution.py:108
  35.0 14.4 %all-to-all-start.1 = ((bf16[2,1,1024,128]{3,0,1,2:T(2,128)(2,1)}), bf16[2,1,1024,128]{3,0,1,2:T(2,128)(2,1)S(1)}, u32[]{:S(2)}, u32[]{:S(2)}) async-start(bf16[2,1,1024,128]{3,0,1,2:T(2,128)(2,1)} %copy.107), calls=%async_computation.1 | async-start | bytes 1048576 | tf_op jit(solution)/shard_map/all_to_all | solution.py:106
  49.4 14.4 %all-to-all-start = ((bf16[2,1,1024,128]{3,0,1,2:T(2,128)(2,1)}), bf16[2,1,1024,128]{3,0,1,2:T(2,128)(2,1)S(1)}, u32[]{:S(2)}, u32[]{:S(2)}) async-start(bf16[2,1,1024,128]{3,0,1,2:T(2,128)(2,1)} %copy.105), calls=%async_computation | async-start | bytes 1048576 | tf_op jit(solution)/shard_map/all_to_all | solution.py:105
  63.8 16.2 %all-to-all-start.3 = ((bf16[2,1,1024,128]{3,0,1,2:T(2,128)(2,1)}), bf16[2,1,1024,128]{3,0,1,2:T(2,128)(2,1)}, u32[]{:S(2)}, u32[]{:S(2)}) async-start(bf16[2,1,1024,128]{3,0,1,2:T(2,128)(2,1)} %copy.113), calls=%async_computation.3 | async-start | bytes 1048576 | tf_op jit(solution)/shard_map/all_to_all | solution.py:107
  80.0 9.8 %copy-start.5 = (f32[2,64,16,16]{2,3,1,0:T(8,128)}, f32[2,64,16,16]{2,3,1,0:T(8,128)S(1)}, u32[]{:S(2)}) copy-start(f32[2,64,16,16]{2,3,1,0:T(8,128)S(1)} %get-tuple-element.33) | copy-start | bytes 393220
  84.1 15.6 %all-to-all-start.5 = ((bf16[2,16,64,128]{3,2,0,1:T(8,128)(2,1)}), bf16[2,16,64,128]{3,2,0,1:T(8,128)(2,1)S(1)}, u32[]{:S(2)}, u32[]{:S(2)}) async-start(bf16[2,16,64,128]{3,2,0,1:T(8,128)(2,1)} %copy.123), calls=%async_computation.5 | async-start | bytes 1048576 | tf_op jit(solution)/shard_map/all_to_all | solution.py:116
  96.8 12.2 %copy-start.4 = (bf16[2,1024,128]{2,1,0:T(8,128)(2,1)S(1)}, bf16[2,1024,128]{2,1,0:T(8,128)(2,1)}, u32[]{:S(2)}) copy-start(bf16[2,1024,128]{2,1,0:T(8,128)(2,1)} %param.10) | copy-start | bytes 1572868
  96.8 16.5 %copy-start.3 = (bf16[2,1,1024,128]{3,2,0,1:T(8,128)(2,1)S(1)}, bf16[2,1,1024,128]{3,2,0,1:T(8,128)(2,1)}, u32[]{:S(2)}) copy-start(bf16[2,1,1024,128]{3,2,0,1:T(8,128)(2,1)} %copy.112) | copy-start | bytes 1572868
  99.7 15.1 %all-to-all-start.6 = ((bf16[2,16,64,128]{3,2,0,1:T(8,128)(2,1)}), bf16[2,16,64,128]{3,2,0,1:T(8,128)(2,1)S(1)}, u32[]{:S(2)}, u32[]{:S(2)}) async-start(bf16[2,16,64,128]{3,2,0,1:T(8,128)(2,1)} %copy.126), calls=%async_computation.6 | async-start | bytes 1048576 | tf_op jit(solution)/shard_map/all_to_all | solution.py:117
  104.2 9.1 %copy-start.6 = (f32[2,64,16,16]{2,3,1,0:T(8,128)S(1)}, f32[2,64,16,16]{2,3,1,0:T(8,128)}, u32[]{:S(2)}) copy-start(f32[2,64,16,16]{2,3,1,0:T(8,128)} %copy-done.5) | copy-start | bytes 393220
  104.2 16.3 %copy-start.2 = (bf16[2,1024,128]{2,1,0:T(8,128)(2,1)S(1)}, bf16[2,1024,128]{2,1,0:T(8,128)(2,1)}, u32[]{:S(2)}) copy-start(bf16[2,1024,128]{2,1,0:T(8,128)(2,1)} %param.14) | copy-start | bytes 1572868
  114.7 15.6 %all-to-all-start.7 = ((bf16[2,16,64,128]{3,2,0,1:T(8,128)(2,1)}), bf16[2,16,64,128]{3,2,0,1:T(8,128)(2,1)S(1)}, u32[]{:S(2)}, u32[]{:S(2)}) async-start(bf16[2,16,64,128]{3,2,0,1:T(8,128)(2,1)} %copy.129), calls=%async_computation.7 | async-start | bytes 1048576 | tf_op jit(solution)/shard_map/all_to_all | solution.py:118
where the time goes:
time: 132 us; the launch traced here: 131 us
  starting transfers between devices  42.2 us (32%)
  waiting for transfers between devices  35.1 us (27%)
  matrix products  33.5 us (25%)
  local copies, waits for them, and re-layouts  16.4 us (12%)
  other arithmetic  3.19 us (2%)
    all_to_all x1, waiting for transfers between devices, body(): lax.all_to_all(payload[0], 'frames', split_axis=2, concat_axis=1, tiled=T...  8.54 us
    unnamed x18, local copies, waits for them, and re-layouts  8.49 us
    all_to_all x1, waiting for transfers between devices, body(): lax.all_to_all(payload[3], 'frames', split_axis=2, concat_axis=1, tiled=T...  7.51 us
    all_to_all x1, waiting for transfers between devices, body(): lax.all_to_all(payload[1], 'frames', split_axis=2, concat_axis=1, tiled=T...  7.51 us
    all_to_all x1, waiting for transfers between devices, body(): lax.all_to_all(payload[4], 'frames', split_axis=2, concat_axis=1, tiled=T...  7.43 us
    all_to_all x1, starting transfers between devices, body(): lax.all_to_all(payload[4], 'frames', split_axis=2, concat_axis=1, tiled=T...  7.34 us
    sub x1, matrix products, spatial_grads(): weights = jax.nn.softmax(scores, axis=-1)  7 us
    dot_general x1, matrix products, spatial_grads(): jnp.einsum('fqhd,fkhd->fhqk', grad_heads, value_heads, preferred_element_...  6.95 us
  transfers between devices with their start and end apart: 8, of which 6 were waited for; matrix products, arithmetic and copies ran while one was open for 35% of the time, Pallas kernels for 0%

commit v1 on v0

v1 whole, which is shorter than its diff:
```python
import functools
import math

import jax
import jax.numpy as jnp
from jax import lax
from jax.experimental import pallas as pl
from jax.experimental.pallas import tpu as pltpu
from jax.sharding import PartitionSpec as P

HD = 128
QB = 256
TG = 16
SCALE = HD**-0.5
EXP2_SCALE = SCALE * math.log2(math.e)


def dot(a, b, contract_a, contract_b):
    return lax.dot_general(
        a, b, (((contract_a,), (contract_b,)), ((), ())), preferred_element_type=jnp.float32
    )


def softmax(scores):
    top = jnp.max(scores, axis=-1, keepdims=True)
    powers = jnp.exp2((scores - top) * EXP2_SCALE)
    return powers * (1.0 / jnp.sum(powers, axis=-1, keepdims=True))


def kernel(
    n,
    qs_hbm, ks_hbm, vs_hbm, os_hbm, gs_hbm,
    qt_hbm, kt_hbm, vt_hbm, ot_hbm, gt_hbm,
    dqs_hbm, dks_hbm, dvs_hbm, dqt_hbm, dkt_hbm, dvt_hbm,
    spatial_in, spatial_out, dk_sum, dv_sum, stat_in, stats, stats_got, arrived, leaving,
    in_sem, out_sem, stat_in_sem, stat_send, stat_recv, go_send, go_recv, back_send, back_recv,
):
    me = lax.axis_index("frames")
    clips, _, tokens, _ = qt_hbm.shape
    part = tokens // n
    mine = pl.ds(pl.multiple_of(me * part, part), part)
    payload = (qt_hbm, kt_hbm, vt_hbm, gt_hbm)
    results = (dqt_hbm, dkt_hbm, dvt_hbm)

    def peer(step):
        return lax.rem(me + step, n)

    stat_loads = []
    for i, ref in enumerate((gt_hbm, ot_hbm)):
        copy = pltpu.make_async_copy(ref.at[:, 0], stat_in.at[i], stat_in_sem.at[i])
        copy.start()
        stat_loads.append(copy)
    loads = []
    for f in range(clips):
        group = []
        for i, ref in enumerate((qs_hbm, ks_hbm, vs_hbm, os_hbm, gs_hbm)):
            copy = pltpu.make_async_copy(ref.at[f], spatial_in.at[i, f], in_sem.at[i, f])
            copy.start()
            group.append(copy)
        loads.append(group)

    barrier = pltpu.get_barrier_semaphore()

    def greet(step, carry):
        pl.semaphore_signal(barrier, inc=1, device_id={"frames": peer(step)})
        return carry

    lax.fori_loop(1, n, greet, 0)
    pl.semaphore_wait(barrier, n - 1)

    def go(c):
        def one(step, carry):
            to = peer(step)
            rows = pl.ds(pl.multiple_of(to * part, part), part)
            for a, ref in enumerate(payload):
                pltpu.make_async_remote_copy(
                    src_ref=ref.at[c, 0, rows],
                    dst_ref=arrived.at[c, a, me],
                    send_sem=go_send.at[c],
                    recv_sem=go_recv.at[c],
                    device_id={"frames": to},
                ).start()
            return carry

        lax.fori_loop(1, n, one, 0)
        for a, ref in enumerate(payload):
            pltpu.make_async_copy(
                ref.at[c, 0, mine], arrived.at[c, a, me], go_recv.at[c]
            ).start()

    go(0)
    go(1)

    for copy in stat_loads:
        copy.wait()
    blocks = tokens // HD
    eye = lax.broadcasted_iota(jnp.int32, (HD, HD), 0) == lax.broadcasted_iota(
        jnp.int32, (HD, HD), 1
    )
    for c in range(clips):
        for b in range(blocks):
            rows = slice(b * HD, (b + 1) * HD)
            products = stat_in[0, c, rows].astype(jnp.float32) * stat_in[1, c, rows].astype(
                jnp.float32
            )
            sums = jnp.sum(products, axis=-1, keepdims=True)
            row = jnp.sum(jnp.where(eye, sums, 0.0), axis=0, keepdims=True)
            stats[b, c : c + 1] = row.astype(jnp.bfloat16).astype(jnp.float32)

    per_block = HD // part

    def send_stats(step, carry):
        to = peer(step)
        pltpu.make_async_remote_copy(
            src_ref=stats.at[to // per_block],
            dst_ref=stats_got.at[me],
            send_sem=stat_send,
            recv_sem=stat_recv,
            device_id={"frames": to},
        ).start()
        return carry

    lax.fori_loop(1, n, send_stats, 0)
    pltpu.make_async_copy(stats.at[me // per_block], stats_got.at[me], stat_recv).start()

    def spatial(f):
        for copy in loads[f]:
            copy.wait()
        keys = spatial_in[1, f]
        values = spatial_in[2, f]
        for i in range(tokens // QB):
            rows = slice(i * QB, (i + 1) * QB)
            query = spatial_in[0, f, rows]
            grad = spatial_in[4, f, rows]
            rowdot = jnp.sum(
                grad.astype(jnp.float32) * spatial_in[3, f, rows].astype(jnp.float32),
                axis=-1,
                keepdims=True,
            )
            weights = softmax(dot(query, keys, 1, 1))
            dweights = dot(grad, values, 1, 1)
            dscores = (weights * (dweights - rowdot)).astype(jnp.bfloat16)
            dv = dot(weights.astype(jnp.bfloat16), grad, 0, 0)
            dk = dot(dscores, query, 0, 0)
            if i:
                dv = dv + dv_sum[...]
                dk = dk + dk_sum[...]
            if i < tokens // QB - 1:
                dv_sum[...] = dv
                dk_sum[...] = dk
            else:
                spatial_out[2, f] = dv.astype(jnp.bfloat16)
                spatial_out[1, f] = (dk * SCALE).astype(jnp.bfloat16)
            spatial_out[0, f, rows] = (dot(dscores, keys, 1, 0) * SCALE).astype(jnp.bfloat16)
        copies = []
        for i, ref in enumerate((dqs_hbm, dks_hbm, dvs_hbm)):
            copy = pltpu.make_async_copy(spatial_out.at[i, f], ref.at[f], out_sem.at[i, f])
            copy.start()
            copies.append(copy)
        return copies

    side = n * TG
    same_token = (
        lax.broadcasted_iota(jnp.int32, (side, side), 0) % TG
        == lax.broadcasted_iota(jnp.int32, (side, side), 1) % TG
    )

    def temporal(c):
        pltpu.make_async_copy(arrived.at[c], arrived.at[c], go_recv.at[c]).wait()
        if c == 0:
            pltpu.make_async_copy(stats_got, stats_got, stat_recv).wait()
        row_stats = (
            jnp.broadcast_to(stats_got[:, c : c + 1], (n, TG, HD))
            .reshape(side, HD)
            .astype(jnp.bfloat16)
        )
        lane = lax.broadcasted_iota(jnp.int32, (side, HD), 1)
        token = lax.broadcasted_iota(jnp.int32, (side, HD), 0) % TG
        first = lax.rem(me, per_block) * part
        for g in range(part // TG):
            rows = slice(g * TG, (g + 1) * TG)
            query = arrived[c, 0, :, rows].reshape(side, HD)
            keys = arrived[c, 1, :, rows].reshape(side, HD)
            values = arrived[c, 2, :, rows].reshape(side, HD)
            grad = arrived[c, 3, :, rows].reshape(side, HD)
            pick = jnp.where(lane == first + g * TG + token, -1.0, 0.0).astype(jnp.bfloat16)
            weights = softmax(jnp.where(same_token, dot(query, keys, 1, 1), -1e30))
            shifted = dot(grad, values, 1, 1) + dot(row_stats, pick, 1, 1)
            dscores = (weights * shifted).astype(jnp.bfloat16)
            dv = dot(weights.astype(jnp.bfloat16), grad, 0, 0)
            dq = dot(dscores, keys, 1, 0) * SCALE
            dk = dot(dscores, query, 0, 0) * SCALE
            for a, value in enumerate((dq, dk, dv)):
                leaving[c, a, :, rows] = value.astype(jnp.bfloat16).reshape(n, TG, HD)

        def one(step, carry):
            to = peer(step)
            for a, ref in enumerate(results):
                pltpu.make_async_remote_copy(
                    src_ref=leaving.at[c, a, to],
                    dst_ref=ref.at[c, 0, mine],
                    send_sem=back_send.at[a],
                    recv_sem=back_recv.at[a],
                    device_id={"frames": to},
                ).start()
            return carry

        lax.fori_loop(1, n, one, 0)
        for a, ref in enumerate(results):
            pltpu.make_async_copy(
                leaving.at[c, a, me], ref.at[c, 0, mine], back_recv.at[a]
            ).start()

    copies = spatial(0)
    temporal(0)
    copies += spatial(1)
    temporal(1)

    for copy in copies:
        copy.wait()
    for c in range(clips):
        sent = arrived.at[c, :, pl.ds(0, n - 1)]
        pltpu.make_async_copy(sent, sent, go_send.at[c]).wait()
    sent = stats_got.at[pl.ds(0, n - 1)]
    pltpu.make_async_copy(sent, sent, stat_send).wait()
    for a, ref in enumerate(results):
        sent = leaving.at[:, a, pl.ds(0, n - 1)]
        pltpu.make_async_copy(sent, sent, back_send.at[a]).wait()
        pltpu.make_async_copy(ref, ref, back_recv.at[a]).wait()


def body(*args):
    n = lax.axis_size("frames")
    spatial, temporal = args[0], args[5]
    frames, tokens, _ = spatial.shape
    clips = temporal.shape[0]
    part = tokens // n
    hbm = pl.BlockSpec(memory_space=pltpu.HBM)
    out_shape = [jax.ShapeDtypeStruct(spatial.shape, jnp.bfloat16)] * 3 + [
        jax.ShapeDtypeStruct(temporal.shape, jnp.bfloat16)
    ] * 3
    dma = pltpu.SemaphoreType.DMA
    return tuple(
        pl.pallas_call(
            functools.partial(kernel, n),
            out_shape=out_shape,
            in_specs=[hbm] * 10,
            out_specs=[hbm] * 6,
            scratch_shapes=[
                pltpu.VMEM((5, frames, tokens, HD), jnp.bfloat16),
                pltpu.VMEM((3, frames, tokens, HD), jnp.bfloat16),
                pltpu.VMEM((tokens, HD), jnp.float32),
                pltpu.VMEM((tokens, HD), jnp.float32),
                pltpu.VMEM((2, clips, tokens, HD), jnp.bfloat16),
                pltpu.VMEM((tokens // HD, clips, HD), jnp.float32),
                pltpu.VMEM((n, clips, HD), jnp.float32),
                pltpu.VMEM((clips, 4, n, part, HD), jnp.bfloat16),
                pltpu.VMEM((clips, 3, n, part, HD), jnp.bfloat16),
                dma((5, frames)),
                dma((3, frames)),
                dma((2,)),
                dma,
                dma,
                dma((clips,)),
                dma((clips,)),
                dma((3,)),
                dma((3,)),
            ],
            compiler_params=pltpu.CompilerParams(
                collective_id=0, has_side_effects=True, vmem_limit_bytes=56 * 2**20
            ),
            cost_estimate=pl.CostEstimate(
                flops=5 * 2 * frames * tokens * tokens * HD,
                bytes_accessed=16 * frames * tokens * HD * 2,
                transcendentals=frames * tokens * tokens,
            ),
        )(*args)
    )


def solution(mesh):
    spatial = P("frames", None, "heads")
    temporal = P(None, "frames", None, "heads")
    return jax.shard_map(
        body,
        mesh=mesh,
        in_specs=(spatial,) * 5 + (temporal,) * 5,
        out_specs=(spatial,) * 3 + (temporal,) * 3,
        check_vma=False,
    )
```

time: 132 us -> 66.2 us (0.50)
  Pallas kernels: 0 us -> 57.6 us
  starting transfers between devices: 42.2 us -> 0 us
  waiting for transfers between devices: 35.1 us -> 0 us
  matrix products: 33.5 us -> 0 us
  local copies, waits for them, and re-layouts: 16.4 us -> 7.64 us
  other arithmetic: 3.19 us -> 0 us
    pallas_call x0 -> x1, Pallas kernels: none -> 57.6 us  [body(): pl.pallas_call(functools.partial(kernel, n), out_shape=out_shape, in_spec...]
    all_to_all x8 -> x0, starting transfers between devices: 42.2 us -> none  [the longest x1 7.34 us: body(): lax.all_to_all(payload[4], 'frames', split_axis=2, concat_axis=1, tiled=T...]
    all_to_all x8 -> x0, waiting for transfers between devices: 35.1 us -> none  [the longest x1 8.54 us: body(): lax.all_to_all(payload[0], 'frames', split_axis=2, concat_axis=1, tiled=T...]
    dot_general x8 -> x0, matrix products: 25.5 us -> none  [the longest x1 6.95 us: spatial_grads(): jnp.einsum('fqhd,fkhd->fhqk', grad_heads, value_heads, preferred_element_...]
    sub x2 -> x0, matrix products: 7.99 us -> none  [the longest x1 7 us: spatial_grads(): weights = jax.nn.softmax(scores, axis=-1)]
    all_to_all x7 -> x0, local copies, waits for them, and re-layouts: 3.82 us -> none  [the longest x1 0.88 us: body(): lax.all_to_all(payload[3], 'frames', split_axis=2, concat_axis=1, tiled=T...]
    reduce_sum x2 -> x0, other arithmetic: 3.19 us -> none  [the longest x1 1.64 us: row_statistic(): jnp.sum(products.reshape(clip_count, frames, columns, channels // HD, HD)...]
    reshape x3 -> x0, local copies, waits for them, and re-layouts: 2.81 us -> none  [the longest x1 0.94 us: temporal_grads(): grad_value.reshape(final)]
  transfers between devices with their start and end apart: 8 -> 0, of which waited for: 6 -> 0; matrix products, arithmetic and copies ran while one was open for 35% -> 0% of each run, Pallas kernels for 0% -> 0%
where the time goes in v1:
time: 66.2 us; the launch traced here: 65.9 us
  Pallas kernels  57.6 us (87%)
  local copies, waits for them, and re-layouts  7.64 us (12%)
    pallas_call x1, Pallas kernels, body(): pl.pallas_call(functools.partial(kernel, n), out_shape=out_shape, in_spec...  57.6 us
    unnamed x16, local copies, waits for them, and re-layouts  7.64 us

profile of v1, /device:TPU:1, one launch (start us, length us, event | category | flops | bytes accessed | tf_op | source)
XLA Modules:
  0.0 65.9 jit_solution(15163131968070595013)
XLA Ops:
  0.6 57.6 %shard_map.145 = (bf16[2,1024,128]{2,1,0:T(8,128)(2,1)}, bf16[2,1024,128]{2,1,0:T(8,128)(2,1)}, bf16[2,1024,128]{2,1,0:T(8,128)(2,1)}, bf16[2,1,1024,128]{3,2,1,...) custom-call(bf16[2,1024,128]{2,1,0:T(8,128)(2,1)} %qs_hbm.1, ...), custom_call_target="tpu_custom_call" | custom-call | flops 2684354560 | bytes 8388608 | tf_op jit(solution)/shard_map/pallas_call | solution.py:244
  58.2 0.0 copy-start.4
  58.2 1.9 %copy.22 = bf16[2,1024,128]{2,1,0:T(8,128)(2,1)} copy(bf16[2,1024,128]{2,1,0:T(8,128)(2,1)} %get-tuple-element.12) | data formatting | bytes 1048576
  60.1 0.0 copy-done.4
  60.1 0.0 copy-start.3
  60.1 0.8 %copy.23 = bf16[2,1024,128]{2,1,0:T(8,128)(2,1)} copy(bf16[2,1024,128]{2,1,0:T(8,128)(2,1)S(1)} %copy-done.4) | data formatting | bytes 1048576
  60.9 0.4 copy-done.3
  61.4 0.0 copy-start.2
  61.4 0.8 %copy.24 = bf16[2,1024,128]{2,1,0:T(8,128)(2,1)} copy(bf16[2,1024,128]{2,1,0:T(8,128)(2,1)S(1)} %copy-done.3) | data formatting | bytes 1048576
  62.2 0.4 copy-done.2
  62.6 0.0 copy-start.1
  62.6 0.8 %copy.25 = bf16[2,1,1024,128]{3,2,1,0:T(8,128)(2,1)} copy(bf16[2,1,1024,128]{3,2,1,0:T(8,128)(2,1)S(1)} %copy-done.2) | data formatting | bytes 1048576
  63.4 0.4 copy-done.1
  63.8 0.0 copy-start
  63.8 0.8 %copy.26 = bf16[2,1,1024,128]{3,2,1,0:T(8,128)(2,1)} copy(bf16[2,1,1024,128]{3,2,1,0:T(8,128)(2,1)S(1)} %copy-done.1) | data formatting | bytes 1048576
  64.6 0.4 copy-done
  65.1 0.8 %copy.27 = bf16[2,1,1024,128]{3,2,1,0:T(8,128)(2,1)} copy(bf16[2,1,1024,128]{3,2,1,0:T(8,128)(2,1)S(1)} %copy-done) | data formatting | bytes 1048576
Async XLA Ops:
  58.2 1.9 %copy-start.4 = (bf16[2,1024,128]{2,1,0:T(8,128)(2,1)S(1)}, bf16[2,1024,128]{2,1,0:T(8,128)(2,1)}, u32[]{:S(2)}) copy-start(bf16[2,1024,128]{2,1,0:T(8,128)(2,1)} %get-tuple-element.13) | copy-start | bytes 1572868
  60.1 1.2 %copy-start.3 = (bf16[2,1024,128]{2,1,0:T(8,128)(2,1)S(1)}, bf16[2,1024,128]{2,1,0:T(8,128)(2,1)}, u32[]{:S(2)}) copy-start(bf16[2,1024,128]{2,1,0:T(8,128)(2,1)} %get-tuple-element.14) | copy-start | bytes 1572868
  61.4 1.2 %copy-start.2 = (bf16[2,1,1024,128]{3,2,1,0:T(8,128)(2,1)S(1)}, bf16[2,1,1024,128]{3,2,1,0:T(8,128)(2,1)}, u32[]{:S(2)}) copy-start(bf16[2,1,1024,128]{3,2,1,0:T(8,128)(2,1)} %get-tuple-element.15) | copy-start | bytes 1572868
  62.6 1.2 %copy-start.1 = (bf16[2,1,1024,128]{3,2,1,0:T(8,128)(2,1)S(1)}, bf16[2,1,1024,128]{3,2,1,0:T(8,128)(2,1)}, u32[]{:S(2)}) copy-start(bf16[2,1,1024,128]{3,2,1,0:T(8,128)(2,1)} %get-tuple-element.16) | copy-start | bytes 1572868
  63.8 1.2 %copy-start = (bf16[2,1,1024,128]{3,2,1,0:T(8,128)(2,1)S(1)}, bf16[2,1,1024,128]{3,2,1,0:T(8,128)(2,1)}, u32[]{:S(2)}) copy-start(bf16[2,1,1024,128]{3,2,1,0:T(8,128)(2,1)} %get-tuple-element.17) | copy-start | bytes 1572868

commit v2 on v1

--- a/solution.py
+++ b/solution.py
@@ -12,6 +12,10 @@
 QB = 256
 TG = 16
 SCALE = HD**-0.5
+STEPS = (
+    (1, 2, 0), (1, 2, 1), (1, 1, 0), (1, 3, 1), (1, 3, 0), (1, 1, 1), (0, 2, 0), (1, 0, 1),
+    (0, 2, 1), (1, 0, 0), (0, 1, 0), (0, 3, 1), (0, 3, 0), (0, 1, 1), (0, 0, 1),
+)
 EXP2_SCALE = SCALE * math.log2(math.e)
 
 
@@ -42,8 +46,11 @@
     payload = (qt_hbm, kt_hbm, vt_hbm, gt_hbm)
     results = (dqt_hbm, dkt_hbm, dvt_hbm)
 
-    def peer(step):
-        return lax.rem(me + step, n)
+    z, y, core = me // 8, lax.rem(me // 2, 4), lax.rem(me, 2)
+    peers = [
+        lax.rem(z + dz, 2) * 8 + lax.rem(y + dy, 4) * 2 + lax.rem(core + dc, 2)
+        for dz, dy, dc in STEPS
+    ]
 
     stat_loads = []
     for i, ref in enumerate((gt_hbm, ot_hbm)):
@@ -61,18 +68,14 @@
 
     barrier = pltpu.get_barrier_semaphore()
 
-    def greet(step, carry):
-        pl.semaphore_signal(barrier, inc=1, device_id={"frames": peer(step)})
-        return carry
-
-    lax.fori_loop(1, n, greet, 0)
+    for to in peers:
+        pl.semaphore_signal(barrier, inc=1, device_id={"frames": to})
     pl.semaphore_wait(barrier, n - 1)
 
     def go(c):
-        def one(step, carry):
-            to = peer(step)
-            rows = pl.ds(pl.multiple_of(to * part, part), part)
-            for a, ref in enumerate(payload):
+        for a, ref in enumerate(payload):
+            for to in peers:
+                rows = pl.ds(pl.multiple_of(to * part, part), part)
                 pltpu.make_async_remote_copy(
                     src_ref=ref.at[c, 0, rows],
                     dst_ref=arrived.at[c, a, me],
@@ -80,16 +83,11 @@
                     recv_sem=go_recv.at[c],
                     device_id={"frames": to},
                 ).start()
-            return carry
-
-        lax.fori_loop(1, n, one, 0)
-        for a, ref in enumerate(payload):
             pltpu.make_async_copy(
                 ref.at[c, 0, mine], arrived.at[c, a, me], go_recv.at[c]
             ).start()
 
     go(0)
-    go(1)
 
     for copy in stat_loads:
         copy.wait()
@@ -109,8 +107,7 @@
 
     per_block = HD // part
 
-    def send_stats(step, carry):
-        to = peer(step)
+    for to in peers:
         pltpu.make_async_remote_copy(
             src_ref=stats.at[to // per_block],
             dst_ref=stats_got.at[me],
@@ -118,10 +115,10 @@
             recv_sem=stat_recv,
             device_id={"frames": to},
         ).start()
-        return carry
-
-    lax.fori_loop(1, n, send_stats, 0)
     pltpu.make_async_copy(stats.at[me // per_block], stats_got.at[me], stat_recv).start()
+
+    for c in range(1, clips):
+        go(c)
 
     def spatial(f):
         for copy in loads[f]:
@@ -193,9 +190,8 @@
             for a, value in enumerate((dq, dk, dv)):
                 leaving[c, a, :, rows] = value.astype(jnp.bfloat16).reshape(n, TG, HD)
 
-        def one(step, carry):
-            to = peer(step)
-            for a, ref in enumerate(results):
+        for a, ref in enumerate(results):
+            for to in peers:
                 pltpu.make_async_remote_copy(
                     src_ref=leaving.at[c, a, to],
                     dst_ref=ref.at[c, 0, mine],
@@ -203,10 +199,6 @@
                     recv_sem=back_recv.at[a],
                     device_id={"frames": to},
                 ).start()
-            return carry
-
-        lax.fori_loop(1, n, one, 0)
-        for a, ref in enumerate(results):
             pltpu.make_async_copy(
                 leaving.at[c, a, me], ref.at[c, 0, mine], back_recv.at[a]
             ).start()
@@ -229,6 +221,24 @@
         pltpu.make_async_copy(ref, ref, back_recv.at[a]).wait()
 
 
+def write_out(*refs):
+    sources, targets = refs[:6], refs[6:12]
+    held, in_sem, out_sem = refs[12:]
+    halves = held.shape[1]
+    jobs = []
+    for h in range(halves):
+        for i in range(6):
+            load = pltpu.make_async_copy(sources[i].at[h], held.at[i, h], in_sem.at[i, h])
+            load.start()
+            store = pltpu.make_async_copy(held.at[i, h], targets[i].at[h], out_sem.at[i, h])
+            jobs.append((load, store))
+    for load, store in jobs:
+        load.wait()
+        store.start()
+    for load, store in jobs:
+        store.wait()
+
+
 def body(*args):
     n = lax.axis_size("frames")
     spatial, temporal = args[0], args[5]
@@ -240,42 +250,53 @@
         jax.ShapeDtypeStruct(temporal.shape, jnp.bfloat16)
     ] * 3
     dma = pltpu.SemaphoreType.DMA
-    return tuple(
-        pl.pallas_call(
-            functools.partial(kernel, n),
-            out_shape=out_shape,
-            in_specs=[hbm] * 10,
-            out_specs=[hbm] * 6,
-            scratch_shapes=[
-                pltpu.VMEM((5, frames, tokens, HD), jnp.bfloat16),
-                pltpu.VMEM((3, frames, tokens, HD), jnp.bfloat16),
-                pltpu.VMEM((tokens, HD), jnp.float32),
-                pltpu.VMEM((tokens, HD), jnp.float32),
-                pltpu.VMEM((2, clips, tokens, HD), jnp.bfloat16),
-                pltpu.VMEM((tokens // HD, clips, HD), jnp.float32),
-                pltpu.VMEM((n, clips, HD), jnp.float32),
-                pltpu.VMEM((clips, 4, n, part, HD), jnp.bfloat16),
-                pltpu.VMEM((clips, 3, n, part, HD), jnp.bfloat16),
-                dma((5, frames)),
-                dma((3, frames)),
-                dma((2,)),
-                dma,
-                dma,
-                dma((clips,)),
-                dma((clips,)),
-                dma((3,)),
-                dma((3,)),
-            ],
-            compiler_params=pltpu.CompilerParams(
-                collective_id=0, has_side_effects=True, vmem_limit_bytes=56 * 2**20
-            ),
-            cost_estimate=pl.CostEstimate(
-                flops=5 * 2 * frames * tokens * tokens * HD,
-                bytes_accessed=16 * frames * tokens * HD * 2,
-                transcendentals=frames * tokens * tokens,
-            ),
-        )(*args)
-    )
+    gradients = pl.pallas_call(
+        functools.partial(kernel, n),
+        out_shape=out_shape,
+        in_specs=[hbm] * 10,
+        out_specs=[hbm] * 6,
+        scratch_shapes=[
+            pltpu.VMEM((5, frames, tokens, HD), jnp.bfloat16),
+            pltpu.VMEM((3, frames, tokens, HD), jnp.bfloat16),
+            pltpu.VMEM((tokens, HD), jnp.float32),
+            pltpu.VMEM((tokens, HD), jnp.float32),
+            pltpu.VMEM((2, clips, tokens, HD), jnp.bfloat16),
+            pltpu.VMEM((tokens // HD, clips, HD), jnp.float32),
+            pltpu.VMEM((n, clips, HD), jnp.float32),
+            pltpu.VMEM((clips, 4, n, part, HD), jnp.bfloat16),
+            pltpu.VMEM((clips, 3, n, part, HD), jnp.bfloat16),
+            dma((5, frames)),
+            dma((3, frames)),
+            dma((2,)),
+            dma,
+            dma,
+            dma((clips,)),
+            dma((clips,)),
+            dma((3,)),
+            dma((3,)),
+        ],
+        compiler_params=pltpu.CompilerParams(
+            collective_id=0, has_side_effects=True, vmem_limit_bytes=56 * 2**20
+        ),
+        cost_estimate=pl.CostEstimate(
+            flops=5 * 2 * frames * tokens * tokens * HD,
+            bytes_accessed=16 * frames * tokens * HD * 2,
+            transcendentals=frames * tokens * tokens,
+        ),
+    )(*args)
+    flat = [g.reshape(spatial.shape) for g in gradients]
+    written = pl.pallas_call(
+        write_out,
+        out_shape=out_shape[:1] * 6,
+        in_specs=[hbm] * 6,
+        out_specs=[hbm] * 6,
+        scratch_shapes=[
+            pltpu.VMEM((6, frames, tokens, HD), jnp.bfloat16),
+            dma((6, frames)),
+            dma((6, frames)),
+        ],
+    )(*flat)
+    return tuple(g.reshape(o.shape) for o, g in zip(out_shape, written))
 
 
 def solution(mesh):

time: 66.2 us -> 51.3 us (0.77)
  local copies, waits for them, and re-layouts: 7.64 us -> 0 us
  Pallas kernels: 57.6 us -> 50.5 us
    pallas_call x1, Pallas kernels: 57.6 us -> 47.7 us  [body(): pl.pallas_call(functools.partial(kernel, n), out_shape=out_shape, in_spec...]
    unnamed x16 -> x0, local copies, waits for them, and re-layouts: 7.64 us -> none
    pallas_call x0 -> x1, Pallas kernels: none -> 2.81 us  [body(): pl.pallas_call(write_out, out_shape=out_shape[:1] * 6, in_specs=[hbm] * 6...]
where the time goes in v2:
time: 51.3 us; the launch traced here: 51.2 us
  Pallas kernels  50.5 us (98%)
  between operations  0.64 us (1%)
    pallas_call x1, Pallas kernels, body(): pl.pallas_call(functools.partial(kernel, n), out_shape=out_shape, in_spec...  47.7 us
    pallas_call x1, Pallas kernels, body(): pl.pallas_call(write_out, out_shape=out_shape[:1] * 6, in_specs=[hbm] * 6...  2.81 us

profile of v2, /device:TPU:1, one launch (start us, length us, event | category | flops | bytes accessed | tf_op | source)
XLA Modules:
  0.0 51.2 jit_solution(5479645295263702820)
XLA Ops:
  0.6 47.7 %shard_map.145 = (bf16[2,1024,128]{2,1,0:T(8,128)(2,1)}, bf16[2,1024,128]{2,1,0:T(8,128)(2,1)}, bf16[2,1024,128]{2,1,0:T(8,128)(2,1)}, bf16[2,1,1024,128]{3,2,1,...) custom-call(bf16[2,1024,128]{2,1,0:T(8,128)(2,1)} %qs_hbm.1, ...), custom_call_target="tpu_custom_call" | custom-call | flops 2684354560 | bytes 8388608 | tf_op jit(solution)/shard_map/pallas_call | solution.py:253
  48.3 2.8 %shard_map.146 = (bf16[2,1024,128]{2,1,0:T(8,128)(2,1)}, bf16[2,1024,128]{2,1,0:T(8,128)(2,1)}, bf16[2,1024,128]{2,1,0:T(8,128)(2,1)}, bf16[2,1024,128]{2,1,0:T(...) custom-call(bf16[2,1024,128]{2,1,0:T(8,128)(2,1)} %get-tuple-element.18.refs_0_, ...), custom_call_target="tpu_custom_call" | custom-call | tf_op jit(solution)/shard_map/pallas_call | solution.py:288

commit v3 on v2

--- a/solution.py
+++ b/solution.py
@@ -11,6 +11,7 @@
 HD = 128
 QB = 256
 TG = 16
+VMEM_LIMIT = 101 * 2**19
 SCALE = HD**-0.5
 STEPS = (
     (1, 2, 0), (1, 2, 1), (1, 1, 0), (1, 3, 1), (1, 3, 0), (1, 1, 1), (0, 2, 0), (1, 0, 1),
@@ -52,6 +53,10 @@
         for dz, dy, dc in STEPS
     ]
 
+    barrier = pltpu.get_barrier_semaphore()
+    for to in peers:
+        pl.semaphore_signal(barrier, inc=1, device_id={"frames": to})
+
     stat_loads = []
     for i, ref in enumerate((gt_hbm, ot_hbm)):
         copy = pltpu.make_async_copy(ref.at[:, 0], stat_in.at[i], stat_in_sem.at[i])
@@ -66,10 +71,6 @@
             group.append(copy)
         loads.append(group)
 
-    barrier = pltpu.get_barrier_semaphore()
-
-    for to in peers:
-        pl.semaphore_signal(barrier, inc=1, device_id={"frames": to})
     pl.semaphore_wait(barrier, n - 1)
 
     def go(c):
@@ -222,21 +223,12 @@
 
 
 def write_out(*refs):
-    sources, targets = refs[:6], refs[6:12]
-    held, in_sem, out_sem = refs[12:]
-    halves = held.shape[1]
-    jobs = []
-    for h in range(halves):
-        for i in range(6):
-            load = pltpu.make_async_copy(sources[i].at[h], held.at[i, h], in_sem.at[i, h])
-            load.start()
-            store = pltpu.make_async_copy(held.at[i, h], targets[i].at[h], out_sem.at[i, h])
-            jobs.append((load, store))
-    for load, store in jobs:
-        load.wait()
-        store.start()
-    for load, store in jobs:
-        store.wait()
+    sources, targets, sem = refs[:6], refs[6:12], refs[12]
+    copies = [pltpu.make_async_copy(sources[i], targets[i], sem.at[i]) for i in range(6)]
+    for copy in copies:
+        copy.start()
+    for copy in copies:
+        copy.wait()
 
 
 def body(*args):
@@ -246,6 +238,7 @@
     clips = temporal.shape[0]
     part = tokens // n
     hbm = pl.BlockSpec(memory_space=pltpu.HBM)
+    anywhere = pl.BlockSpec(memory_space=pl.ANY)
     out_shape = [jax.ShapeDtypeStruct(spatial.shape, jnp.bfloat16)] * 3 + [
         jax.ShapeDtypeStruct(temporal.shape, jnp.bfloat16)
     ] * 3
@@ -254,7 +247,7 @@
         functools.partial(kernel, n),
         out_shape=out_shape,
         in_specs=[hbm] * 10,
-        out_specs=[hbm] * 6,
+        out_specs=[anywhere] * 6,
         scratch_shapes=[
             pltpu.VMEM((5, frames, tokens, HD), jnp.bfloat16),
             pltpu.VMEM((3, frames, tokens, HD), jnp.bfloat16),
@@ -276,7 +269,7 @@
             dma((3,)),
         ],
         compiler_params=pltpu.CompilerParams(
-            collective_id=0, has_side_effects=True, vmem_limit_bytes=56 * 2**20
+            collective_id=0, has_side_effects=True, vmem_limit_bytes=VMEM_LIMIT
         ),
         cost_estimate=pl.CostEstimate(
             flops=5 * 2 * frames * tokens * tokens * HD,
@@ -288,13 +281,10 @@
     written = pl.pallas_call(
         write_out,
         out_shape=out_shape[:1] * 6,
-        in_specs=[hbm] * 6,
+        in_specs=[anywhere] * 6,
         out_specs=[hbm] * 6,
-        scratch_shapes=[
-            pltpu.VMEM((6, frames, tokens, HD), jnp.bfloat16),
-            dma((6, frames)),
-            dma((6, frames)),
-        ],
+        scratch_shapes=[dma((6,))],
+        compiler_params=pltpu.CompilerParams(vmem_limit_bytes=2 * 2**20),
     )(*flat)
     return tuple(g.reshape(o.shape) for o, g in zip(out_shape, written))
 

time: 51.3 us -> 50.2 us (0.979)
  Pallas kernels: 50.5 us -> 49.3 us
    pallas_call x1, Pallas kernels: 2.81 us -> 1.71 us  [body(): pl.pallas_call(write_out, out_shape=out_shape[:1] * 6, in_specs=[anywhere...]
where the time goes in v3:
time: 50.2 us; the launch traced here: 50.1 us
  Pallas kernels  49.3 us (98%)
  between operations  0.8 us (2%)
    pallas_call x1, Pallas kernels, body(): pl.pallas_call(functools.partial(kernel, n), out_shape=out_shape, in_spec...  47.6 us
    pallas_call x1, Pallas kernels, body(): pl.pallas_call(write_out, out_shape=out_shape[:1] * 6, in_specs=[anywhere...  1.71 us

profile of v3, /device:TPU:1, one launch (start us, length us, event | category | flops | bytes accessed | tf_op | source)
XLA Modules:
  0.0 50.1 jit_solution(10426930248046633717)
XLA Ops:
  0.6 47.6 %shard_map.145 = (bf16[2,1024,128]{2,1,0:T(8,128)(2,1)S(1)}, bf16[2,1024,128]{2,1,0:T(8,128)(2,1)S(1)}, bf16[2,1024,128]{2,1,0:T(8,128)(2,1)S(1)}, bf16[2,1,1024...) custom-call(bf16[2,1024,128]{2,1,0:T(8,128)(2,1)} %qs_hbm.1, ...), custom_call_target="tpu_custom_call" | custom-call | flops 2684354560 | bytes 8388608 | tf_op jit(solution)/shard_map/pallas_call | solution.py:246
  48.2 1.7 %shard_map.146 = (bf16[2,1024,128]{2,1,0:T(8,128)(2,1)}, bf16[2,1024,128]{2,1,0:T(8,128)(2,1)}, bf16[2,1024,128]{2,1,0:T(8,128)(2,1)}, bf16[2,1024,128]{2,1,0:T(...) custom-call(bf16[2,1024,128]{2,1,0:T(8,128)(2,1)S(1)} %get-tuple-element.18.refs_0_, ...), custom_call_target="tpu_custom_call" | custom-call | tf_op jit(solution)/shard_map/pallas_call | solution.py:281

commit v4 on v3

--- a/solution.py
+++ b/solution.py
@@ -11,6 +11,11 @@
 HD = 128
 QB = 256
 TG = 16
+VMEM_LIMIT = 101 * 2**19
+SCALE = HD**-0.5
+NEAR = ((1, 0, 0), (0, 1, 0), (0, 3, 0), (1, 0, 1), (0, 1, 1), (0, 3, 1), (0, 0, 1))
+MIDDLE = ((0, 2, 0), (1, 1, 0), (1, 3, 0), (0, 2, 1), (1, 1, 1), (1, 3, 1))
+FAR = ((1, 2, 0), (1, 2, 1))
 VMEM_LIMIT = 101 * 2**19
 SCALE = HD**-0.5
 STEPS = (
@@ -39,6 +44,7 @@
     dqs_hbm, dks_hbm, dvs_hbm, dqt_hbm, dkt_hbm, dvt_hbm,
     spatial_in, spatial_out, dk_sum, dv_sum, stat_in, stats, stats_got, arrived, leaving,
     in_sem, out_sem, stat_in_sem, stat_send, stat_recv, go_send, go_recv, back_send, back_recv,
+    near_sem, middle_sem,
 ):
     me = lax.axis_index("frames")
     clips, _, tokens, _ = qt_hbm.shape
@@ -48,14 +54,40 @@
     results = (dqt_hbm, dkt_hbm, dvt_hbm)
 
     z, y, core = me // 8, lax.rem(me // 2, 4), lax.rem(me, 2)
-    peers = [
-        lax.rem(z + dz, 2) * 8 + lax.rem(y + dy, 4) * 2 + lax.rem(core + dc, 2)
-        for dz, dy, dc in STEPS
-    ]
+
+    def at(step):
+        dz, dy, dc = step
+        return lax.rem(z + dz, 2) * 8 + lax.rem(y + dy, 4) * 2 + lax.rem(core + dc, 2)
+
+    near, middle, far = ([at(step) for step in steps] for steps in (NEAR, MIDDLE, FAR))
+    everyone = far + middle + near
 
     barrier = pltpu.get_barrier_semaphore()
-    for to in peers:
+    for to in near:
         pl.semaphore_signal(barrier, inc=1, device_id={"frames": to})
+
+    def go(c, peers):
+        for a, ref in enumerate(payload):
+            for to in peers:
+                rows = pl.ds(pl.multiple_of(to * part, part), part)
+                pltpu.make_async_remote_copy(
+                    src_ref=ref.at[c, 0, rows],
+                    dst_ref=arrived.at[c, a, me],
+                    send_sem=go_send.at[c],
+                    recv_sem=go_recv.at[c],
+                    device_id={"frames": to},
+                ).start()
+
+    def stay(c):
+        for a, ref in enumerate(payload):
+            pltpu.make_async_copy(
+                ref.at[c, 0, mine], arrived.at[c, a, me], go_recv.at[c]
+            ).start()
+
+    pl.semaphore_wait(barrier, len(NEAR))
+    for step in NEAR[:3]:
+        pl.semaphore_signal(near_sem, inc=1, device_id={"frames": at(step)})
+    go(0, near)
 
     stat_loads = []
     for i, ref in enumerate((gt_hbm, ot_hbm)):
@@ -71,24 +103,12 @@
             group.append(copy)
         loads.append(group)
 
-    pl.semaphore_wait(barrier, n - 1)
-
-    def go(c):
-        for a, ref in enumerate(payload):
-            for to in peers:
-                rows = pl.ds(pl.multiple_of(to * part, part), part)
-                pltpu.make_async_remote_copy(
-                    src_ref=ref.at[c, 0, rows],
-                    dst_ref=arrived.at[c, a, me],
-                    send_sem=go_send.at[c],
-                    recv_sem=go_recv.at[c],
-                    device_id={"frames": to},
-                ).start()
-            pltpu.make_async_copy(
-                ref.at[c, 0, mine], arrived.at[c, a, me], go_recv.at[c]
-            ).start()
-
-    go(0)
+    stay(0)
+    pl.semaphore_wait(near_sem, 3)
+    pl.semaphore_signal(middle_sem, inc=1, device_id={"frames": at(NEAR[0])})
+    go(0, middle)
+    pl.semaphore_wait(middle_sem, 1)
+    go(0, far)
 
     for copy in stat_loads:
         copy.wait()
@@ -108,7 +128,7 @@
 
     per_block = HD // part
 
-    for to in peers:
+    for to in everyone:
         pltpu.make_async_remote_copy(
             src_ref=stats.at[to // per_block],
             dst_ref=stats_got.at[me],
@@ -119,7 +139,8 @@
     pltpu.make_async_copy(stats.at[me // per_block], stats_got.at[me], stat_recv).start()
 
     for c in range(1, clips):
-        go(c)
+        go(c, everyone)
+        stay(c)
 
     def spatial(f):
         for copy in loads[f]:
@@ -191,15 +212,18 @@
             for a, value in enumerate((dq, dk, dv)):
                 leaving[c, a, :, rows] = value.astype(jnp.bfloat16).reshape(n, TG, HD)
 
+        sends = [(a, to) for a in range(len(results)) for to in everyone]
+        if c == clips - 1:
+            sends = [(a, to) for to in everyone for a in range(len(results))]
+        for a, to in sends:
+            pltpu.make_async_remote_copy(
+                src_ref=leaving.at[c, a, to],
+                dst_ref=results[a].at[c, 0, mine],
+                send_sem=back_send.at[a],
+                recv_sem=back_recv.at[a],
+                device_id={"frames": to},
+            ).start()
         for a, ref in enumerate(results):
-            for to in peers:
-                pltpu.make_async_remote_copy(
-                    src_ref=leaving.at[c, a, to],
-                    dst_ref=ref.at[c, 0, mine],
-                    send_sem=back_send.at[a],
-                    recv_sem=back_recv.at[a],
-                    device_id={"frames": to},
-                ).start()
             pltpu.make_async_copy(
                 leaving.at[c, a, me], ref.at[c, 0, mine], back_recv.at[a]
             ).start()
@@ -267,6 +291,8 @@
             dma((clips,)),
             dma((3,)),
             dma((3,)),
+            pltpu.SemaphoreType.REGULAR,
+            pltpu.SemaphoreType.REGULAR,
         ],
         compiler_params=pltpu.CompilerParams(
             collective_id=0, has_side_effects=True, vmem_limit_bytes=VMEM_LIMIT

time: 50.2 us -> 49.7 us (0.990)
  no operation moved by 1% of the time
where the time goes in v4:
time: 49.7 us; the launch traced here: 49.6 us
  Pallas kernels  48.8 us (98%)
  between operations  0.8 us (2%)
    pallas_call x1, Pallas kernels, body(): pl.pallas_call(functools.partial(kernel, n), out_shape=out_shape, in_spec...  47.1 us
    pallas_call x1, Pallas kernels, body(): pl.pallas_call(write_out, out_shape=out_shape[:1] * 6, in_specs=[anywhere...  1.71 us

profile of v4, /device:TPU:1, one launch (start us, length us, event | category | flops | bytes accessed | tf_op | source)
XLA Modules:
  0.0 49.6 jit_solution(14264753329612769294)
XLA Ops:
  0.6 47.1 %shard_map.145 = (bf16[2,1024,128]{2,1,0:T(8,128)(2,1)S(1)}, bf16[2,1024,128]{2,1,0:T(8,128)(2,1)S(1)}, bf16[2,1024,128]{2,1,0:T(8,128)(2,1)S(1)}, bf16[2,1,1024...) custom-call(bf16[2,1024,128]{2,1,0:T(8,128)(2,1)} %qs_hbm.1, ...), custom_call_target="tpu_custom_call" | custom-call | flops 2684354560 | bytes 8388608 | tf_op jit(solution)/shard_map/pallas_call | solution.py:270
  47.7 1.7 %shard_map.146 = (bf16[2,1024,128]{2,1,0:T(8,128)(2,1)}, bf16[2,1024,128]{2,1,0:T(8,128)(2,1)}, bf16[2,1024,128]{2,1,0:T(8,128)(2,1)}, bf16[2,1024,128]{2,1,0:T(...) custom-call(bf16[2,1024,128]{2,1,0:T(8,128)(2,1)S(1)} %get-tuple-element.18.refs_0_, ...), custom_call_target="tpu_custom_call" | custom-call | tf_op jit(solution)/shard_map/pallas_call | solution.py:307

commit v5 on v4

--- a/solution.py
+++ b/solution.py
@@ -85,9 +85,10 @@
             ).start()
 
     pl.semaphore_wait(barrier, len(NEAR))
+    go(0, near[:3])
     for step in NEAR[:3]:
         pl.semaphore_signal(near_sem, inc=1, device_id={"frames": at(step)})
-    go(0, near)
+    go(0, near[3:])
 
     stat_loads = []
     for i, ref in enumerate((gt_hbm, ot_hbm)):
@@ -145,10 +146,12 @@
     def spatial(f):
         for copy in loads[f]:
             copy.wait()
-        keys = spatial_in[1, f]
-        values = spatial_in[2, f]
-        for i in range(tokens // QB):
-            rows = slice(i * QB, (i + 1) * QB)
+        dv_sum[...] = jnp.zeros_like(dv_sum)
+        dk_sum[...] = jnp.zeros_like(dk_sum)
+
+        def step(i, carry):
+            rows = pl.ds(pl.multiple_of(i * QB, QB), QB)
+            keys = spatial_in[1, f]
             query = spatial_in[0, f, rows]
             grad = spatial_in[4, f, rows]
             rowdot = jnp.sum(
@@ -157,20 +160,16 @@
                 keepdims=True,
             )
             weights = softmax(dot(query, keys, 1, 1))
-            dweights = dot(grad, values, 1, 1)
+            dweights = dot(grad, spatial_in[2, f], 1, 1)
             dscores = (weights * (dweights - rowdot)).astype(jnp.bfloat16)
-            dv = dot(weights.astype(jnp.bfloat16), grad, 0, 0)
-            dk = dot(dscores, query, 0, 0)
-            if i:
-                dv = dv + dv_sum[...]
-                dk = dk + dk_sum[...]
-            if i < tokens // QB - 1:
-                dv_sum[...] = dv
-                dk_sum[...] = dk
-            else:
-                spatial_out[2, f] = dv.astype(jnp.bfloat16)
-                spatial_out[1, f] = (dk * SCALE).astype(jnp.bfloat16)
+            dv_sum[...] += dot(weights.astype(jnp.bfloat16), grad, 0, 0)
+            dk_sum[...] += dot(dscores, query, 0, 0)
             spatial_out[0, f, rows] = (dot(dscores, keys, 1, 0) * SCALE).astype(jnp.bfloat16)
+            return carry
+
+        lax.fori_loop(0, tokens // QB, step, 0)
+        spatial_out[2, f] = dv_sum[...].astype(jnp.bfloat16)
+        spatial_out[1, f] = (dk_sum[...] * SCALE).astype(jnp.bfloat16)
         copies = []
         for i, ref in enumerate((dqs_hbm, dks_hbm, dvs_hbm)):
             copy = pltpu.make_async_copy(spatial_out.at[i, f], ref.at[f], out_sem.at[i, f])
@@ -196,8 +195,8 @@
         lane = lax.broadcasted_iota(jnp.int32, (side, HD), 1)
         token = lax.broadcasted_iota(jnp.int32, (side, HD), 0) % TG
         first = lax.rem(me, per_block) * part
-        for g in range(part // TG):
-            rows = slice(g * TG, (g + 1) * TG)
+        def group(g, carry):
+            rows = pl.ds(pl.multiple_of(g * TG, TG), TG)
             query = arrived[c, 0, :, rows].reshape(side, HD)
             keys = arrived[c, 1, :, rows].reshape(side, HD)
             values = arrived[c, 2, :, rows].reshape(side, HD)
@@ -211,6 +210,9 @@
             dk = dot(dscores, query, 0, 0) * SCALE
             for a, value in enumerate((dq, dk, dv)):
                 leaving[c, a, :, rows] = value.astype(jnp.bfloat16).reshape(n, TG, HD)
+            return carry
+
+        lax.fori_loop(0, part // TG, group, 0)
 
         sends = [(a, to) for a in range(len(results)) for to in everyone]
         if c == clips - 1:

time: 49.7 us -> 49.5 us (level)
  no operation moved by 1% of the time
where the time goes in v5:
time: 49.5 us
  Pallas kernels  48.8 us (99%)
  between operations  0.64 us (1%)
    pallas_call x1, Pallas kernels, body(): pl.pallas_call(functools.partial(kernel, n), out_shape=out_shape, in_spec...  47.1 us
    pallas_call x1, Pallas kernels, body(): pl.pallas_call(write_out, out_shape=out_shape[:1] * 6, in_specs=[anywhere...  1.71 us

profile of v5, /device:TPU:1, one launch (start us, length us, event | category | flops | bytes accessed | tf_op | source)
XLA Modules:
  0.0 49.5 jit_solution(4826795736120149923)
XLA Ops:
  0.6 47.1 %shard_map.145 = (bf16[2,1024,128]{2,1,0:T(8,128)(2,1)S(1)}, bf16[2,1024,128]{2,1,0:T(8,128)(2,1)S(1)}, bf16[2,1024,128]{2,1,0:T(8,128)(2,1)S(1)}, bf16[2,1,1024...) custom-call(bf16[2,1024,128]{2,1,0:T(8,128)(2,1)} %qs_hbm.1, ...), custom_call_target="tpu_custom_call" | custom-call | flops 2684354560 | bytes 8388608 | tf_op jit(solution)/shard_map/pallas_call | solution.py:272
  47.7 1.7 %shard_map.146 = (bf16[2,1024,128]{2,1,0:T(8,128)(2,1)}, bf16[2,1024,128]{2,1,0:T(8,128)(2,1)}, bf16[2,1024,128]{2,1,0:T(8,128)(2,1)}, bf16[2,1024,128]{2,1,0:T(...) custom-call(bf16[2,1024,128]{2,1,0:T(8,128)(2,1)S(1)} %get-tuple-element.18.refs_0_, ...), custom_call_target="tpu_custom_call" | custom-call | tf_op jit(solution)/shard_map/pallas_call | solution.py:309

commit v6 on v5

--- a/solution.py
+++ b/solution.py
@@ -95,15 +95,9 @@
         copy = pltpu.make_async_copy(ref.at[:, 0], stat_in.at[i], stat_in_sem.at[i])
         copy.start()
         stat_loads.append(copy)
-    loads = []
     for f in range(clips):
-        group = []
         for i, ref in enumerate((qs_hbm, ks_hbm, vs_hbm, os_hbm, gs_hbm)):
-            copy = pltpu.make_async_copy(ref.at[f], spatial_in.at[i, f], in_sem.at[i, f])
-            copy.start()
-            group.append(copy)
-        loads.append(group)
-
+            pltpu.make_async_copy(ref.at[f], spatial_in.at[i, f], in_sem.at[i, f]).start()
     stay(0)
     pl.semaphore_wait(near_sem, 3)
     pl.semaphore_signal(middle_sem, inc=1, device_id={"frames": at(NEAR[0])})
@@ -144,8 +138,9 @@
         stay(c)
 
     def spatial(f):
-        for copy in loads[f]:
-            copy.wait()
+        for i in range(5):
+            held = spatial_in.at[i, f]
+            pltpu.make_async_copy(held, held, in_sem.at[i, f]).wait()
         dv_sum[...] = jnp.zeros_like(dv_sum)
         dk_sum[...] = jnp.zeros_like(dk_sum)
 
@@ -170,12 +165,8 @@
         lax.fori_loop(0, tokens // QB, step, 0)
         spatial_out[2, f] = dv_sum[...].astype(jnp.bfloat16)
         spatial_out[1, f] = (dk_sum[...] * SCALE).astype(jnp.bfloat16)
-        copies = []
         for i, ref in enumerate((dqs_hbm, dks_hbm, dvs_hbm)):
-            copy = pltpu.make_async_copy(spatial_out.at[i, f], ref.at[f], out_sem.at[i, f])
-            copy.start()
-            copies.append(copy)
-        return copies
+            pltpu.make_async_copy(spatial_out.at[i, f], ref.at[f], out_sem.at[i]).start()
 
     side = n * TG
     same_token = (
@@ -185,10 +176,13 @@
 
     def temporal(c):
         pltpu.make_async_copy(arrived.at[c], arrived.at[c], go_recv.at[c]).wait()
-        if c == 0:
+
+        @pl.when(c == 0)
+        def _():
             pltpu.make_async_copy(stats_got, stats_got, stat_recv).wait()
+
         row_stats = (
-            jnp.broadcast_to(stats_got[:, c : c + 1], (n, TG, HD))
+            jnp.broadcast_to(stats_got[:, pl.ds(c, 1)], (n, TG, HD))
             .reshape(side, HD)
             .astype(jnp.bfloat16)
         )
@@ -214,9 +208,7 @@
 
         lax.fori_loop(0, part // TG, group, 0)
 
-        sends = [(a, to) for a in range(len(results)) for to in everyone]
-        if c == clips - 1:
-            sends = [(a, to) for to in everyone for a in range(len(results))]
+        sends = [(a, to) for to in everyone for a in range(len(results))]
         for a, to in sends:
             pltpu.make_async_remote_copy(
                 src_ref=leaving.at[c, a, to],
@@ -230,13 +222,15 @@
                 leaving.at[c, a, me], ref.at[c, 0, mine], back_recv.at[a]
             ).start()
 
-    copies = spatial(0)
-    temporal(0)
-    copies += spatial(1)
-    temporal(1)
-
-    for copy in copies:
-        copy.wait()
+    def both(c, carry):
+        spatial(c)
+        temporal(c)
+        return carry
+
+    lax.fori_loop(0, clips, both, 0)
+
+    for i, ref in enumerate((dqs_hbm, dks_hbm, dvs_hbm)):
+        pltpu.make_async_copy(spatial_out.at[i], ref, out_sem.at[i]).wait()
     for c in range(clips):
         sent = arrived.at[c, :, pl.ds(0, n - 1)]
         pltpu.make_async_copy(sent, sent, go_send.at[c]).wait()
@@ -285,7 +279,7 @@
             pltpu.VMEM((clips, 4, n, part, HD), jnp.bfloat16),
             pltpu.VMEM((clips, 3, n, part, HD), jnp.bfloat16),
             dma((5, frames)),
-            dma((3, frames)),
+            dma((3,)),
             dma((2,)),
             dma,
             dma,

time: 49.5 us -> 51.1 us (1.032)
  Pallas kernels: 48.8 us -> 50.4 us
    pallas_call x1, Pallas kernels: 47.1 us -> 48.7 us  [body(): pl.pallas_call(functools.partial(kernel, n), out_shape=out_shape, in_spec...]
where the time goes in v6:
time: 51.1 us
  Pallas kernels  50.4 us (99%)
  between operations  0.64 us (1%)
    pallas_call x1, Pallas kernels, body(): pl.pallas_call(functools.partial(kernel, n), out_shape=out_shape, in_spec...  48.7 us
    pallas_call x1, Pallas kernels, body(): pl.pallas_call(write_out, out_shape=out_shape[:1] * 6, in_specs=[anywhere...  1.71 us

profile of v6, /device:TPU:1, one launch (start us, length us, event | category | flops | bytes accessed | tf_op | source)
XLA Modules:
  0.0 51.1 jit_solution(11344383578908343669)
XLA Ops:
  0.6 48.7 %shard_map.145 = (bf16[2,1024,128]{2,1,0:T(8,128)(2,1)S(1)}, bf16[2,1024,128]{2,1,0:T(8,128)(2,1)S(1)}, bf16[2,1024,128]{2,1,0:T(8,128)(2,1)S(1)}, bf16[2,1,1024...) custom-call(bf16[2,1024,128]{2,1,0:T(8,128)(2,1)} %qs_hbm.1, ...), custom_call_target="tpu_custom_call" | custom-call | flops 2684354560 | bytes 8388608 | tf_op jit(solution)/shard_map/pallas_call | solution.py:266
  49.3 1.7 %shard_map.146 = (bf16[2,1024,128]{2,1,0:T(8,128)(2,1)}, bf16[2,1024,128]{2,1,0:T(8,128)(2,1)}, bf16[2,1024,128]{2,1,0:T(8,128)(2,1)}, bf16[2,1024,128]{2,1,0:T(...) custom-call(bf16[2,1024,128]{2,1,0:T(8,128)(2,1)S(1)} %get-tuple-element.18.refs_0_, ...), custom_call_target="tpu_custom_call" | custom-call | tf_op jit(solution)/shard_map/pallas_call | solution.py:303
